TPU v7x, 32 devices: a whole 2x2x4 slice. The times are simulated.
32 devices in a mesh: feat: 2 (over y), rows: 16 (over z, x, core).
Axes of the slice: x: 2, y: 2, z: 4, core: 2. Of those that a mesh axis runs over, the one named last changes fastest.
Arguments:
- features: bfloat16 [4096, 2048], P('rows', 'feat'), may hold values from -6 to 6
- labels: int32 [4096], P('rows'), may hold values from 0 to 639
- inv_gram: float32 [2, 1024, 1024], P('feat'), may hold values from -1 to 1, as said below
Outputs:
- weights: float32 [2048, 640], P(('feat', 'rows'))
- after_block: float32 [2, 4096, 640], P('feat', 'rows')
Inputs may be any that keep to these rules, and one draw needn't show every extreme that they name: Each of the 2 matrices of inv_gram is symmetric.
All inputs are finite; a program needn't handle non-finite values.
Results may differ from a plain program's by a relative error of at most 0.0094.
Values sent between devices are 32-bit elements; how exact they have to be, the bound alone decides.
A program may use at most 64 MiB of HBM per device.

v0:
```python
import jax
import jax.numpy as jnp
from jax import lax
from jax.sharding import PartitionSpec as P

C = 640
CLS_BLK = 128


def shifted(value, axis, by):
    count = lax.axis_size(axis)
    pairs = [(i, i + by) for i in range(count) if 0 <= i + by < count]
    return lax.ppermute(value, axis, pairs)


def local(features, labels, inv_gram):
    rows_here = features.shape[0]
    block_width = features.shape[1]
    group_total = lax.axis_size("feat")
    shard_total = lax.axis_size("rows")
    feat_index = lax.axis_index("feat")
    shard_index = lax.axis_index("rows")
    row_share = block_width // shard_total
    class_block = CLS_BLK
    wave_total = C // class_block
    class_ids = jnp.arange(C, dtype=jnp.int32)
    onehot = (labels[:, None] == class_ids[None, :]).astype(jnp.float32)
    counts = lax.psum(jnp.sum(onehot, axis=0), "rows")
    count_row = jnp.sum(onehot * counts[None, :], axis=1)
    row_weight = float(rows_here * shard_total) / (C * count_row)
    inverse = inv_gram[0]
    residual = jnp.where(feat_index == 0, onehot, jnp.zeros_like(onehot))
    solved_all = jnp.zeros((row_share, C), jnp.float32)
    own_first = shard_index * row_share
    for segment in range(group_total + wave_total - 1):
        wave_index = segment - feat_index
        active = (wave_index >= 0) & (wave_index < wave_total)
        column_start = jnp.clip(wave_index, 0, wave_total - 1) * class_block
        current = lax.dynamic_slice_in_dim(residual, column_start, class_block, 1)
        scaled = (row_weight[:, None] * current).astype(jnp.bfloat16)
        own_sums = lax.psum_scatter(
            lax.dot_general(
                features, scaled, (((0,), (0,)), ((), ())), preferred_element_type=jnp.float32
            ),
            "rows",
            scatter_dimension=0,
            tiled=True,
        )
        solved = jnp.dot(
            inverse,
            lax.all_gather(own_sums, "rows", axis=0, tiled=True),
            precision=lax.Precision.HIGHEST,
            preferred_element_type=jnp.float32,
        )
        correction = jnp.dot(
            features, solved.astype(jnp.bfloat16), preferred_element_type=jnp.float32
        )
        new_rows = lax.dynamic_slice_in_dim(solved, own_first, row_share, 0)
        updated = current - correction
        residual = jnp.where(
            active, lax.dynamic_update_slice_in_dim(residual, updated, column_start, 1), residual
        )
        solved_all = jnp.where(
            active,
            lax.dynamic_update_slice_in_dim(solved_all, new_rows, column_start, 1),
            solved_all,
        )
        arrived = shifted(updated, "feat", 1)
        incoming = segment - feat_index + 1
        landing = (feat_index >= 1) & (incoming >= 0) & (incoming < wave_total)
        landing_start = jnp.clip(incoming, 0, wave_total - 1) * class_block
        residual = jnp.where(
            landing, lax.dynamic_update_slice_in_dim(residual, arrived, landing_start, 1), residual
        )
    return (solved_all, residual[None])


def solution(mesh):
    in_specs = (P("rows", "feat"), P("rows"), P("feat", None, None))
    out_specs = (P(("feat", "rows"), None), P("feat", "rows", None))
    return jax.shard_map(local, mesh=mesh, in_specs=in_specs, out_specs=out_specs, check_vma=False)
```

profile of v0, /device:TPU:7, one launch (start us, length us, event | category | flops | bytes accessed | tf_op | source)
XLA Modules:
  0.0 591.2 jit_solution(534591924117478672)
XLA Ops:
  7.2 0.9 convert_reduce_fusion
  8.1 25.3 %psum.7 = f32[640]{0:T(1024)S(1)} all-reduce(f32[640]{0:T(1024)S(1)} %convert_reduce_fusion), channel_id=1, replica_groups=mesh['feat'=2,'rows'=16] {'rows'}, use_global_device_ids=true, to_apply=%region_1.0 | all-reduce | flops 640 | bytes 5120 | tf_op jit(solution)/shard_map/psum | solution.py:28
  33.4 0.9 select_reduce_fusion
  34.4 0.2 convolution_bitcast_fusion.5
  34.6 1.0 copy.15
  35.6 0.0 reduce-scatter.21.cloned.1.call-start
  35.7 59.1 %reduce-scatter.19.cloned.1.call-done = f32[64,128]{1,0:T(8,128)} async-done(((f32[1024,128]{1,0:T(8,128)}), f32[64,128]{1,0:T(8,128)}) %reduce-scatter.19.cloned.1.call-update) | async-done | bytes 32784 | tf_op jit(solution)/shard_map/reduce_scatter | solution.py:41
  94.8 21.9 %all_gather.18 = f32[1024,128]{1,0:T(8,128)S(1)} all-gather(f32[64,128]{1,0:T(8,128)} %reduce-scatter.19.cloned.1.call-done), channel_id=1, replica_groups=mesh['feat'=2,'rows'=16] {'rows'}, dimensions={0}, use_global_device_ids=true | all-gather | bytes 557056 | tf_op jit(solution)/shard_map/all_gather | solution.py:51
  116.7 6.8 %fusion.10 = f32[128,1024]{1,0:T(8,128)S(1)} fusion(f32[1024,128]{1,0:T(8,128)S(1)} %all_gather.18, f32[1,1024,1024]{2,1,0:T(8,128)} %param.5), kind=kOutput, calls=%fused_computation.10 | convolution fusion | flops 1610612736 | bytes 5242880 | tf_op jit(solution)/shard_map/dot_general | solution.py:49
  123.4 0.3 fusion.17
  123.8 1.3 collective-permute-start
  125.1 5.5 collective-permute-done
  130.6 0.2 convolution_bitcast_fusion.4
  130.9 1.0 copy.17
  131.9 0.0 reduce-scatter.23.cloned.1.call-start
  131.9 53.1 %reduce-scatter.21.cloned.1.call-done = f32[64,128]{1,0:T(8,128)} async-done(((f32[1024,128]{1,0:T(8,128)}), f32[64,128]{1,0:T(8,128)}) %reduce-scatter.21.cloned.1.call-update) | async-done | bytes 32784 | tf_op jit(solution)/shard_map/reduce_scatter | solution.py:41
  185.1 21.9 %all_gather.19 = f32[1024,128]{1,0:T(8,128)S(1)} all-gather(f32[64,128]{1,0:T(8,128)} %reduce-scatter.21.cloned.1.call-done), channel_id=1, replica_groups=mesh['feat'=2,'rows'=16] {'rows'}, dimensions={0}, use_global_device_ids=true | all-gather | bytes 557056 | tf_op jit(solution)/shard_map/all_gather | solution.py:51
  206.9 6.8 %fusion.8 = f32[128,1024]{1,0:T(8,128)S(1)} fusion(f32[1024,128]{1,0:T(8,128)S(1)} %all_gather.19, f32[1,1024,1024]{2,1,0:T(8,128)} %param.5), kind=kOutput, calls=%fused_computation.8 | convolution fusion | flops 1610612736 | bytes 5242880 | tf_op jit(solution)/shard_map/dot_general | solution.py:49
  213.7 0.3 fusion.16
  214.0 1.3 collective-permute-start.1
  215.4 5.5 collective-permute-done.1
  220.9 0.2 convolution_bitcast_fusion.3
  221.2 1.0 copy.19
  222.2 0.0 reduce-scatter.25.cloned.1.call-start
  222.2 53.1 %reduce-scatter.23.cloned.1.call-done = f32[64,128]{1,0:T(8,128)} async-done(((f32[1024,128]{1,0:T(8,128)}), f32[64,128]{1,0:T(8,128)}) %reduce-scatter.23.cloned.1.call-update) | async-done | bytes 32784 | tf_op jit(solution)/shard_map/reduce_scatter | solution.py:41
  275.3 22.1 %all_gather.20 = f32[1024,128]{1,0:T(8,128)S(1)} all-gather(f32[64,128]{1,0:T(8,128)} %reduce-scatter.23.cloned.1.call-done), channel_id=1, replica_groups=mesh['feat'=2,'rows'=16] {'rows'}, dimensions={0}, use_global_device_ids=true | all-gather | bytes 557056 | tf_op jit(solution)/shard_map/all_gather | solution.py:51
  297.4 6.8 %fusion.6 = f32[128,1024]{1,0:T(8,128)S(1)} fusion(f32[1024,128]{1,0:T(8,128)S(1)} %all_gather.20, f32[1,1024,1024]{2,1,0:T(8,128)} %param.5), kind=kOutput, calls=%fused_computation.6 | convolution fusion | flops 1610612736 | bytes 5242880 | tf_op jit(solution)/shard_map/dot_general | solution.py:49
  304.2 0.3 fusion.15
  304.5 1.3 collective-permute-start.2
  305.8 5.5 collective-permute-done.2
  311.4 0.2 convolution_bitcast_fusion.2
  311.6 1.0 copy.21
  312.6 0.0 reduce-scatter.27.cloned.1.call-start
  312.7 53.3 %reduce-scatter.25.cloned.1.call-done = f32[64,128]{1,0:T(8,128)} async-done(((f32[1024,128]{1,0:T(8,128)}), f32[64,128]{1,0:T(8,128)}) %reduce-scatter.25.cloned.1.call-update) | async-done | bytes 32784 | tf_op jit(solution)/shard_map/reduce_scatter | solution.py:41
  365.9 21.8 %all_gather.21 = f32[1024,128]{1,0:T(8,128)S(1)} all-gather(f32[64,128]{1,0:T(8,128)} %reduce-scatter.25.cloned.1.call-done), channel_id=1, replica_groups=mesh['feat'=2,'rows'=16] {'rows'}, dimensions={0}, use_global_device_ids=true | all-gather | bytes 557056 | tf_op jit(solution)/shard_map/all_gather | solution.py:51
  387.7 6.8 %fusion.4 = f32[128,1024]{1,0:T(8,128)S(1)} fusion(f32[1024,128]{1,0:T(8,128)S(1)} %all_gather.21, f32[1,1024,1024]{2,1,0:T(8,128)} %param.5), kind=kOutput, calls=%fused_computation.4 | convolution fusion | flops 1610612736 | bytes 5242880 | tf_op jit(solution)/shard_map/dot_general | solution.py:49
  394.5 0.3 fusion.14
  394.8 1.3 collective-permute-start.3
  396.2 5.5 collective-permute-done.3
  401.7 0.2 convolution_bitcast_fusion.1
  402.0 1.0 copy.23
  403.0 0.0 reduce-scatter.29.cloned.1.call-start
  403.0 53.2 %reduce-scatter.27.cloned.1.call-done = f32[64,128]{1,0:T(8,128)} async-done(((f32[1024,128]{1,0:T(8,128)}), f32[64,128]{1,0:T(8,128)}) %reduce-scatter.27.cloned.1.call-update) | async-done | bytes 32784 | tf_op jit(solution)/shard_map/reduce_scatter | solution.py:41
  456.2 22.0 %all_gather.22 = f32[1024,128]{1,0:T(8,128)S(1)} all-gather(f32[64,128]{1,0:T(8,128)} %reduce-scatter.27.cloned.1.call-done), channel_id=1, replica_groups=mesh['feat'=2,'rows'=16] {'rows'}, dimensions={0}, use_global_device_ids=true | all-gather | bytes 557056 | tf_op jit(solution)/shard_map/all_gather | solution.py:51
  478.2 6.8 %fusion.2 = f32[128,1024]{1,0:T(8,128)S(1)} fusion(f32[1024,128]{1,0:T(8,128)S(1)} %all_gather.22, f32[1,1024,1024]{2,1,0:T(8,128)} %param.5), kind=kOutput, calls=%fused_computation.2 | convolution fusion | flops 1610612736 | bytes 5242880 | tf_op jit(solution)/shard_map/dot_general | solution.py:49
  485.0 0.3 fusion.13
  485.3 1.3 collective-permute-start.4
  486.7 5.5 collective-permute-done.4
  492.2 0.2 convolution_bitcast_fusion
  492.5 1.0 copy.25
  493.5 0.1 bitcast_dynamic-update-slice_fusion.1
  493.6 0.1 fusion.28
  493.7 0.1 fusion.27
  493.8 0.9 fusion.26
  494.7 0.9 fusion.25
  495.7 50.9 %reduce-scatter.29.cloned.1.call-done = f32[64,128]{1,0:T(8,128)} async-done(((f32[1024,128]{1,0:T(8,128)}), f32[64,128]{1,0:T(8,128)}) %reduce-scatter.29.cloned.1.call-update) | async-done | bytes 32784 | tf_op jit(solution)/shard_map/reduce_scatter | solution.py:41
  546.6 21.9 %all_gather.23 = f32[1024,128]{1,0:T(8,128)S(1)} all-gather(f32[64,128]{1,0:T(8,128)} %reduce-scatter.29.cloned.1.call-done), channel_id=1, replica_groups=mesh['feat'=2,'rows'=16] {'rows'}, dimensions={0}, use_global_device_ids=true | all-gather | bytes 557056 | tf_op jit(solution)/shard_map/all_gather | solution.py:51
  568.5 6.7 %fusion = f32[128,1024]{1,0:T(8,128)S(1)} fusion(f32[1024,128]{1,0:T(8,128)S(1)} %all_gather.23, f32[1,1024,1024]{2,1,0:T(8,128)} %param.5), kind=kOutput, calls=%fused_computation | convolution fusion | flops 1610612736 | bytes 5242880 | tf_op jit(solution)/shard_map/dot_general | solution.py:49
  575.2 0.3 fusion.12
  575.5 0.1 fusion.24
  575.6 0.8 copy.13
  576.4 1.3 collective-permute-start.5
  577.8 5.5 collective-permute-done.5
  583.3 1.1 copy.14
  (28 shorter events, 0.5 us)
Async XLA Ops:
  7.2 27.2 %copy-start = (bf16[256,1024]{1,0:T(8,128)(2,1)S(1)}, bf16[256,1024]{1,0:T(8,128)(2,1)}, u32[]{:S(2)}) copy-start(bf16[256,1024]{1,0:T(8,128)(2,1)} %param.3) | copy-start | bytes 1572868
  7.2 87.6 %reduce-scatter.19.cloned.1.call-start = ((), (), s32[]{:S(2)}) async-start(), calls=%async_computation.6 | async-start | bytes 557056 | tf_op jit(solution)/shard_map/reduce_scatter | solution.py:41
  35.6 149.4 %reduce-scatter.21.cloned.1.call-start = ((), (), s32[]{:S(2)}) async-start(), calls=%async_computation.7 | async-start | bytes 557056 | tf_op jit(solution)/shard_map/reduce_scatter | solution.py:41
  123.8 6.8 %collective-permute-start = (f32[256,128]{0,1:T(8,128)S(1)}, f32[256,128]{0,1:T(8,128)S(1)}, u32[]{:S(2)}, u32[]{:S(2)}) collective-permute-start(f32[256,128]{0,1:T(8,128)S(1)} %fusion.17), channel_id=1, source_target_pairs={{0,16},{1,17},{2,18},{3,19},{4,20},{5,21},{6,22},{7,23},{8,24},{9,... | collective-permute-start | bytes 393224 | tf_op jit(solution)/shard_map/ppermute | solution.py:13
  131.9 143.5 %reduce-scatter.23.cloned.1.call-start = ((), (), s32[]{:S(2)}) async-start(), calls=%async_computation.8 | async-start | bytes 557056 | tf_op jit(solution)/shard_map/reduce_scatter | solution.py:41
  214.0 6.8 %collective-permute-start.1 = (f32[256,128]{0,1:T(8,128)S(1)}, f32[256,128]{0,1:T(8,128)S(1)}, u32[]{:S(2)}, u32[]{:S(2)}) collective-permute-start(f32[256,128]{0,1:T(8,128)S(1)} %fusion.16), channel_id=1, source_target_pairs={{0,16},{1,17},{2,18},{3,19},{4,20},{5,21},{6,22},{7,23},{8,24},{9,... | collective-permute-start | bytes 393224 | tf_op jit(solution)/shard_map/ppermute | solution.py:13
  222.2 143.8 %reduce-scatter.25.cloned.1.call-start = ((), (), s32[]{:S(2)}) async-start(), calls=%async_computation.9 | async-start | bytes 557056 | tf_op jit(solution)/shard_map/reduce_scatter | solution.py:41
  304.5 6.8 %collective-permute-start.2 = (f32[256,128]{0,1:T(8,128)S(1)}, f32[256,128]{0,1:T(8,128)S(1)}, u32[]{:S(2)}, u32[]{:S(2)}) collective-permute-start(f32[256,128]{0,1:T(8,128)S(1)} %fusion.15), channel_id=1, source_target_pairs={{0,16},{1,17},{2,18},{3,19},{4,20},{5,21},{6,22},{7,23},{8,24},{9,... | collective-permute-start | bytes 393224 | tf_op jit(solution)/shard_map/ppermute | solution.py:13
  312.6 143.6 %reduce-scatter.27.cloned.1.call-start = ((), (), s32[]{:S(2)}) async-start(), calls=%async_computation.10 | async-start | bytes 557056 | tf_op jit(solution)/shard_map/reduce_scatter | solution.py:41
  394.5 7.2 %copy-start.1 = (f32[128,1024]{1,0:T(8,128)}, f32[128,1024]{1,0:T(8,128)S(1)}, u32[]{:S(2)}) copy-start(f32[128,1024]{1,0:T(8,128)S(1)} %fusion.4) | copy-start | bytes 1572868
  394.8 6.8 %collective-permute-start.3 = (f32[256,128]{0,1:T(8,128)S(1)}, f32[256,128]{0,1:T(8,128)S(1)}, u32[]{:S(2)}, u32[]{:S(2)}) collective-permute-start(f32[256,128]{0,1:T(8,128)S(1)} %fusion.14), channel_id=1, source_target_pairs={{0,16},{1,17},{2,18},{3,19},{4,20},{5,21},{6,22},{7,23},{8,24},{9,... | collective-permute-start | bytes 393224 | tf_op jit(solution)/shard_map/ppermute | solution.py:13
  403.0 143.7 %reduce-scatter.29.cloned.1.call-start = ((), (), s32[]{:S(2)}) async-start(), calls=%async_computation.11 | async-start | bytes 557056 | tf_op jit(solution)/shard_map/reduce_scatter | solution.py:41
  485.0 7.2 %copy-start.2 = (f32[128,1024]{1,0:T(8,128)}, f32[128,1024]{1,0:T(8,128)S(1)}, u32[]{:S(2)}) copy-start(f32[128,1024]{1,0:T(8,128)S(1)} %fusion.2) | copy-start | bytes 1572868
  485.3 6.8 %collective-permute-start.4 = (f32[256,128]{0,1:T(8,128)S(1)}, f32[256,128]{0,1:T(8,128)S(1)}, u32[]{:S(2)}, u32[]{:S(2)}) collective-permute-start(f32[256,128]{0,1:T(8,128)S(1)} %fusion.13), channel_id=1, source_target_pairs={{0,16},{1,17},{2,18},{3,19},{4,20},{5,21},{6,22},{7,23},{8,24},{9,... | collective-permute-start | bytes 393224 | tf_op jit(solution)/shard_map/ppermute | solution.py:13
  576.4 6.8 %collective-permute-start.5 = (f32[256,128]{0,1:T(8,128)S(1)}, f32[256,128]{0,1:T(8,128)S(1)}, u32[]{:S(2)}, u32[]{:S(2)}) collective-permute-start(f32[256,128]{0,1:T(8,128)S(1)} %fusion.12), channel_id=1, source_target_pairs={{0,16},{1,17},{2,18},{3,19},{4,20},{5,21},{6,22},{7,23},{8,24},{9,... | collective-permute-start | bytes 393224 | tf_op jit(solution)/shard_map/ppermute | solution.py:13
Sparse Core Ops, SparseCore 0:
  35.7 59.0 reduce-scatter.18
  132.0 53.0 reduce-scatter.20
  222.3 52.9 reduce-scatter.22
  312.7 53.1 reduce-scatter.24
  403.1 53.1 reduce-scatter.26
  493.6 52.9 reduce-scatter.28
where the time goes:
time: 594 us; the launch traced here: 591 us
  waiting for transfers between devices  356 us (60%)
  blocking collectives  157 us (26%)
  matrix products  43.8 us (7%)
  between operations  14.6 us (2%)
  starting transfers between devices  7.98 us (1%)
  local copies, waits for them, and re-layouts  7.94 us (1%)
    reduce_scatter x6, waiting for transfers between devices, local(): lax.psum_scatter(lax.dot_general(features, scaled, (((0,), (0,)), ((), ()...  323 us
    all_gather x6, blocking collectives, local(): lax.all_gather(own_sums, 'rows', axis=0, tiled=True)  131 us
    dot_general x6, matrix products, local(): jnp.dot(inverse, lax.all_gather(own_sums, 'rows', axis=0, tiled=True), pr...  40.5 us
    ppermute x6, waiting for transfers between devices, shifted(): return lax.ppermute(value, axis, pairs)  33 us
    psum x1, blocking collectives, local(): counts = lax.psum(jnp.sum(onehot, axis=0), 'rows')  25.3 us
  transfers between devices with their start and end apart: 12, of which 12 were waited for; matrix products, arithmetic and copies ran while one was open for 0% of the time, Pallas kernels for 0%

commit v1 on v0

v1 whole, which is shorter than its diff:
```python
import functools
import math

import jax
import jax.numpy as jnp
from jax import lax
from jax.experimental import pallas as pl
from jax.experimental.pallas import tpu as pltpu
from jax.sharding import PartitionSpec as P

C = 640
CHUNK = 128
CORES = 2
MESH = pl.DeviceIdType.MESH


def split(value):
    high = value.astype(jnp.bfloat16)
    return high, (value - high.astype(jnp.float32)).astype(jnp.bfloat16)


def kernel(
    groups, total_rows, order,
    x_ref, labels_ref, inv_ref, w_ref, out_ref,
    inv, xt, m_high, m_low, part, core_in, sum1, inner_in, sum2, outer_in, full, resid, after,
    row_weight, scale, cnt, cnt_core, cnt_inner, cnt_outer,
    inv_sem, cs, cr, xs, xr, zs, zr, zgs, zgr, xgs, xgr, cgs, cgr, ys, yr, ncs, ncr, nxs, nxr, nzs, nzr,
):
    n_feat, n_out, n_in = groups
    feat = lax.axis_index("feat")
    me = lax.axis_index("rows")
    core = lax.rem(me, CORES)
    inner = lax.rem(me // CORES, n_in)
    outer = me // (CORES * n_in)
    rows, width = x_ref.shape
    share = part.shape[-2]
    chunks = part.shape[0]

    def device(o, i, c):
        return (feat, (o * n_in + i) * CORES + c)

    sibling = device(outer, inner, 1 - core)

    def inner_at(d):
        return lax.rem(inner + d, n_in)

    def outer_at(d):
        return lax.rem(outer + d, n_out)

    def remote(src, dst, send, recv, where):
        return pltpu.make_async_remote_copy(
            src_ref=src, dst_ref=dst, send_sem=send, recv_sem=recv, device_id=where, device_id_type=MESH
        )

    inv_copy = pltpu.make_async_copy(inv_ref, inv, inv_sem)
    inv_copy.start()

    barrier = pltpu.get_barrier_semaphore()
    peers = [sibling]
    peers += [device(outer, inner_at(d), core) for d in range(1, n_in)]
    peers += [device(outer_at(d), inner, core) for d in range(1, n_out)]
    for peer in peers:
        pl.semaphore_signal(barrier, inc=1, device_id=peer, device_id_type=MESH)

    @pl.when(feat < n_feat - 1)
    def _():
        pl.semaphore_signal(barrier, inc=1, device_id=(feat + 1, me), device_id_type=MESH)

    @pl.when(feat > 0)
    def _():
        pl.semaphore_signal(barrier, inc=1, device_id=(feat - 1, me), device_id_type=MESH)

    labels = labels_ref[...]
    onehot = (labels == lax.broadcasted_iota(jnp.int32, (rows, C), 1)).astype(jnp.float32)
    cnt[0] = jnp.broadcast_to(jnp.sum(onehot, axis=0, keepdims=True), (8, C))

    @pl.when(feat == 0)
    def _():
        for k in range(chunks):
            resid[k] = onehot[:, k * CHUNK:(k + 1) * CHUNK]

    xt[...] = x_ref[...].T

    beside = (feat < n_feat - 1).astype(jnp.int32) + (feat > 0).astype(jnp.int32)
    pl.semaphore_wait(barrier, len(peers) + beside)

    n_core = remote(cnt.at[0], cnt_core, ncs, ncr, sibling)
    n_core.start()
    n_inner = [
        remote(cnt.at[1], cnt_inner.at[d - 1], nxs.at[d - 1], nxr.at[d - 1], device(outer, inner_at(d), core))
        for d in range(1, n_in)
    ]
    n_outer = [
        remote(cnt.at[2], cnt_outer.at[d - 1], nzs.at[d - 1], nzr.at[d - 1], device(outer_at(d), inner, core))
        for d in range(1, n_out)
    ]

    def count_core():
        n_core.wait_recv()
        cnt[1] = cnt[0] + cnt_core[...]
        for copy in n_inner:
            copy.start()

    def count_inner():
        total = cnt[1]
        for d, copy in enumerate(n_inner):
            copy.wait_recv()
            total = total + cnt_inner[d]
        cnt[2] = total
        for copy in n_outer:
            copy.start()

    def count_outer():
        total = cnt[2]
        for d, copy in enumerate(n_outer):
            copy.wait_recv()
            total = total + cnt_outer[d]
        return total

    def weights_of_classes():
        counts = count_outer()
        by_class = jnp.where(counts > 0, total_rows / (C * jnp.maximum(counts, 1.0)), 0.0)
        scale[...] = by_class.astype(jnp.bfloat16).astype(jnp.float32)

    def weights_of_rows():
        counts = count_outer()
        hot = (labels_ref[...] == lax.broadcasted_iota(jnp.int32, (rows, C), 1)).astype(jnp.float32)
        count_row = jnp.sum(hot * counts[0:1], axis=1, keepdims=True)
        row_weight[...] = total_rows / (C * count_row)
        scale[...] = jnp.ones_like(scale)

    def products():
        inv_copy.wait()
        block = min(256, width)

        @pl.loop(0, width // block)
        def _(j):
            columns = pl.ds(pl.multiple_of(j * block, block), block)
            high, low = split(inv[:, columns])
            x = x_ref[...]
            m = jnp.dot(x, high, preferred_element_type=jnp.float32)
            m = m + jnp.dot(x, low, preferred_element_type=jnp.float32)
            mh, ml = split(m)
            m_high[0:rows, columns] = mh
            m_low[0:rows, columns] = ml

        oh, ol = split(inv[pl.ds(pl.multiple_of(me * share, share), share), :])
        m_high[rows:rows + share, :] = oh
        m_low[rows:rows + share, :] = ol

    to_core, to_inner, to_outer, gather_outer, gather_inner, gather_core, to_next = [], [], [], [], [], [], []
    got_outer, got_inner, got_core = [], [], []
    for k in range(chunks):
        to_core.append(remote(part.at[k, :, :, 1 - core], core_in.at[k], cs.at[k], cr.at[k], sibling))
        to_inner.append([
            remote(sum1.at[k, :, inner_at(d)], inner_in.at[k, d - 1], xs.at[k, d - 1], xr.at[k, d - 1],
                   device(outer, inner_at(d), core))
            for d in range(1, n_in)
        ])
        to_outer.append([
            remote(sum2.at[k, outer_at(d)], outer_in.at[k, d - 1], zs.at[k, d - 1], zr.at[k, d - 1],
                   device(outer_at(d), inner, core))
            for d in range(1, n_out)
        ])
        own = full.at[k, outer, inner, core]
        gather_outer.append([
            remote(own, own, zgs.at[k, d - 1], zgr.at[k, d - 1], device(outer_at(d), inner, core))
            for d in range(1, n_out)
        ])
        got_outer.append([
            remote(own, full.at[k, outer_at(n_out - d), inner, core], zgs.at[k, d - 1], zgr.at[k, d - 1],
                   device(outer_at(d), inner, core))
            for d in range(1, n_out)
        ])
        line = full.at[k, :, inner, core]
        gather_inner.append([
            remote(line, line, xgs.at[k, d - 1], xgr.at[k, d - 1], device(outer, inner_at(d), core))
            for d in range(1, n_in)
        ])
        got_inner.append([
            remote(line, full.at[k, :, inner_at(n_in - d), core], xgs.at[k, d - 1], xgr.at[k, d - 1],
                   device(outer, inner_at(d), core))
            for d in range(1, n_in)
        ])
        half = full.at[k, :, :, core]
        gather_core.append(remote(half, half, cgs.at[k], cgr.at[k], sibling))
        got_core.append(remote(half, full.at[k, :, :, 1 - core], cgs.at[k], cgr.at[k], sibling))
        to_next.append(remote(after.at[k], resid.at[k], ys.at[k], yr.at[k], (lax.rem(feat + 1, n_feat), me)))

    def partial_of(k, scaled):
        value = jnp.dot(xt[...], scaled, preferred_element_type=jnp.float32)
        part[k] = value.reshape(part.shape[1:])
        to_core[k].start()

    def stage_partial(k):
        @pl.when(feat > 0)
        def _():
            to_next[k].wait_recv()
            partial_of(k, (row_weight[...] * resid[k]).astype(jnp.bfloat16))

    def stage_inner(k):
        to_core[k].wait_recv()
        sum1[k] = part[k, :, :, core] + core_in[k]
        for copy in to_inner[k]:
            copy.start()

    def stage_outer(k):
        total = sum1[k, :, inner]
        for d, copy in enumerate(to_inner[k]):
            copy.wait_recv()
            total = total + inner_in[k, d]
        sum2[k] = total
        for copy in to_outer[k]:
            copy.start()

    def stage_own(k):
        total = sum2[k, outer]
        for d, copy in enumerate(to_outer[k]):
            copy.wait_recv()
            total = total + outer_in[k, d]
        full[k, outer, inner, core] = total * scale[0:1, k * CHUNK:(k + 1) * CHUNK]
        for copy in gather_outer[k]:
            copy.start()

    def stage_gather_inner(k):
        for copy in got_outer[k]:
            copy.wait_recv()
        for copy in gather_inner[k]:
            copy.start()

    def stage_gather_core(k):
        for copy in got_inner[k]:
            copy.wait_recv()
        gather_core[k].start()

    def stage_update(k):
        got_core[k].wait_recv()
        high, low = split(full[k].reshape(width, CHUNK))
        mh = m_high[...]
        value = jnp.dot(mh, high, preferred_element_type=jnp.float32)
        value = value + jnp.dot(mh, low, preferred_element_type=jnp.float32)
        value = value + jnp.dot(m_low[...], high, preferred_element_type=jnp.float32)
        updated = resid[k] - value[0:rows]
        after[k] = updated

        @pl.when(feat < n_feat - 1)
        def _():
            to_next[k].start()

        out_ref[0, :, k * CHUNK:(k + 1) * CHUNK] = updated
        w_ref[:, k * CHUNK:(k + 1) * CHUNK] = value[rows:rows + share]

    @pl.when(feat == 0)
    def _():
        for k in range(chunks):
            partial_of(k, resid[k].astype(jnp.bfloat16))

    count_core()

    @pl.when(feat > 0)
    def _():
        count_inner()
        weights_of_rows()
        products()

    stages = [
        stage_partial, stage_inner, stage_outer, stage_own, stage_gather_inner, stage_gather_core, stage_update,
    ]
    for s, k in order:
        if (s, k) == (3, 0):
            @pl.when(feat == 0)
            def _():
                weights_of_classes()
        stages[s](k)
        if (s, k) == (1, 0):
            @pl.when(feat == 0)
            def _():
                count_inner()
        if (s, k) == (2, 0):
            @pl.when(feat == 0)
            def _():
                products()

    n_core.wait_send()
    for copy in n_inner + n_outer:
        copy.wait_send()
    for k in range(chunks):
        for copy in [to_core[k], gather_core[k]] + to_inner[k] + to_outer[k] + gather_outer[k] + gather_inner[k]:
            copy.wait_send()

    @pl.when(feat < n_feat - 1)
    def _():
        for k in range(chunks):
            to_next[k].wait_send()


def solution(mesh):
    n_feat = mesh.shape["feat"]
    n_rows = mesh.shape["rows"]
    n_out = math.gcd(4, n_rows // CORES)
    n_in = n_rows // CORES // n_out
    chunks = C // CHUNK
    order = sorted(
        ((s, k) for s in range(7) for k in range(chunks)), key=lambda at: (at[1] + 1.5 * at[0], -at[0])
    )

    def local(features, labels, inv_gram):
        rows, width = features.shape
        share = width // n_rows
        f32, bf16 = jnp.float32, jnp.bfloat16
        dma = pltpu.SemaphoreType.DMA
        vmem = pltpu.VMEM
        near, far = max(n_in - 1, 1), max(n_out - 1, 1)
        piece = (share, CHUNK)
        pair = lambda *shape: [dma(shape), dma(shape)]
        flops = 2 * rows * width * (2 * width + 4 * C)
        return pl.pallas_call(
            functools.partial(kernel, (n_feat, n_out, n_in), float(rows * n_rows), order),
            out_shape=(
                jax.ShapeDtypeStruct((share, C), f32),
                jax.ShapeDtypeStruct((1, rows, C), f32),
            ),
            in_specs=[
                pl.BlockSpec(memory_space=pltpu.VMEM),
                pl.BlockSpec(memory_space=pltpu.VMEM),
                pl.BlockSpec(memory_space=pl.ANY),
            ],
            out_specs=(pl.BlockSpec(memory_space=pltpu.VMEM), pl.BlockSpec(memory_space=pltpu.VMEM)),
            scratch_shapes=[
                vmem((width, width), f32),
                vmem((width, rows), bf16),
                vmem((rows + share, width), bf16),
                vmem((rows + share, width), bf16),
                vmem((chunks, n_out, n_in, CORES) + piece, f32),
                vmem((chunks, n_out, n_in) + piece, f32),
                vmem((chunks, n_out, n_in) + piece, f32),
                vmem((chunks, near, n_out) + piece, f32),
                vmem((chunks, n_out) + piece, f32),
                vmem((chunks, far) + piece, f32),
                vmem((chunks, n_out, n_in, CORES) + piece, f32),
                vmem((chunks, rows, CHUNK), f32),
                vmem((chunks, rows, CHUNK), f32),
                vmem((rows, 1), f32),
                vmem((8, C), f32),
                vmem((3, 8, C), f32),
                vmem((8, C), f32),
                vmem((near, 8, C), f32),
                vmem((far, 8, C), f32),
                dma,
                *pair(chunks), *pair(chunks, near), *pair(chunks, far), *pair(chunks, far), *pair(chunks, near),
                *pair(chunks), *pair(chunks), dma, dma, *pair(near), *pair(far),
            ],
            compiler_params=pltpu.CompilerParams(
                collective_id=0, has_side_effects=True, vmem_limit_bytes=60 * 1024 * 1024
            ),
            cost_estimate=pl.CostEstimate(flops=flops, bytes_accessed=6 << 20, transcendentals=0),
        )(features, labels[:, None], inv_gram[0])

    in_specs = (P("rows", "feat"), P("rows"), P("feat", None, None))
    out_specs = (P(("feat", "rows"), None), P("feat", "rows", None))
    return jax.shard_map(local, mesh=mesh, in_specs=in_specs, out_specs=out_specs, check_vma=False)
```

time: 594 us -> 97.8 us (0.16)
  waiting for transfers between devices: 356 us -> 0 us
  blocking collectives: 157 us -> 0 us
  Pallas kernels: 0 us -> 90.2 us
  matrix products: 43.8 us -> 0 us
  between operations: 14.6 us -> 0.64 us
  starting transfers between devices: 7.98 us -> 0 us
    reduce_scatter x6 -> x0, waiting for transfers between devices: 323 us -> none  [local(): lax.psum_scatter(lax.dot_general(features, scaled, (((0,), (0,)), ((), ()...]
    all_gather x6 -> x0, blocking collectives: 131 us -> none  [local(): lax.all_gather(own_sums, 'rows', axis=0, tiled=True)]
    pallas_call x0 -> x1, Pallas kernels: none -> 90.2 us  [local(): pl.pallas_call(functools.partial(kernel, (n_feat, n_out, n_in), float(row...]
    dot_general x18 -> x0, matrix products: 43.8 us -> none  [the longest x6 40.5 us: local(): jnp.dot(inverse, lax.all_gather(own_sums, 'rows', axis=0, tiled=True), pr...]
    ppermute x6 -> x0, waiting for transfers between devices: 33 us -> none  [shifted(): return lax.ppermute(value, axis, pairs)]
    psum x1 -> x0, blocking collectives: 25.3 us -> none  [local(): counts = lax.psum(jnp.sum(onehot, axis=0), 'rows')]
    ppermute x6 -> x0, starting transfers between devices: 7.74 us -> none  [shifted(): return lax.ppermute(value, axis, pairs)]
  transfers between devices with their start and end apart: 12 -> 0, of which waited for: 12 -> 0; matrix products, arithmetic and copies ran while one was open for 0% -> 0% of each run, Pallas kernels for 0% -> 0%
where the time goes in v1:
time: 97.8 us; the launch traced here: 95.8 us
  Pallas kernels  90.2 us (92%)
  local copies, waits for them, and re-layouts  5.03 us (5%)
    pallas_call x1, Pallas kernels, local(): pl.pallas_call(functools.partial(kernel, (n_feat, n_out, n_in), float(row...  90.2 us
    unnamed x2, local copies, waits for them, and re-layouts  3.56 us

profile of v1, /device:TPU:7, one launch (start us, length us, event | category | flops | bytes accessed | tf_op | source)
XLA Modules:
  0.0 95.8 jit_solution(7077181100086135598)
XLA Ops:
  0.6 1.5 %copy.5.labels_ref = s32[256,1]{1,0:T(8,128)} copy(s32[256,1]{0,1:T(1,128)} %bitcast.2) | data formatting | bytes 2048 | tf_op jit(solution)/shard_map/broadcast_in_dim | solution.py:357
  2.1 90.2 %shard_map.50 = (f32[64,640]{1,0:T(8,128)}, f32[1,256,640]{2,1,0:T(8,128)}) custom-call(bf16[256,1024]{1,0:T(8,128)(2,1)} %x_ref.1, s32[256,1]{1,0:T(8,128)} %copy.5.labels_ref, f32[1024,1024]{1,0:T(8,128)} %bitcast.3), custom_call_target="tpu_custom_call" | custom-call | flops 2415919104 | bytes 6291456 | tf_op jit(solution)/shard_map/pallas_call | solution.py:317
  92.3 1.6 %copy.8 = f32[64,640]{1,0:T(8,128)} copy(f32[64,640]{1,0:T(8,128)} %get-tuple-element.4) | data formatting | bytes 327680
  93.9 2.0 %copy.9 = f32[1,256,640]{2,1,0:T(8,128)} copy(f32[1,256,640]{2,1,0:T(8,128)} %get-tuple-element.5) | data formatting | bytes 1310720

commit v2 on v1

--- a/solution.py
+++ b/solution.py
@@ -301,7 +301,7 @@
     n_in = n_rows // CORES // n_out
     chunks = C // CHUNK
     order = sorted(
-        ((s, k) for s in range(7) for k in range(chunks)), key=lambda at: (at[1] + 1.5 * at[0], -at[0])
+        ((s, k) for s in range(7) for k in range(chunks)), key=lambda at: (1.0 * at[1] + at[0], -at[0])
     )
 
     def local(features, labels, inv_gram):

time: 97.8 us -> 92.8 us (0.949); the launches traced: 95.8 us -> 92.5 us
  Pallas kernels: 90.2 us -> 86.9 us
    pallas_call x1, Pallas kernels: 90.2 us -> 86.9 us  [local(): pl.pallas_call(functools.partial(kernel, (n_feat, n_out, n_in), float(row...]
where the time goes in v2:
time: 92.8 us; the launch traced here: 92.5 us
  Pallas kernels  86.9 us (94%)
  local copies, waits for them, and re-layouts  5.03 us (5%)
    pallas_call x1, Pallas kernels, local(): pl.pallas_call(functools.partial(kernel, (n_feat, n_out, n_in), float(row...  86.9 us
    unnamed x2, local copies, waits for them, and re-layouts  3.56 us

profile of v2, /device:TPU:7, one launch (start us, length us, event | category | flops | bytes accessed | tf_op | source)
XLA Modules:
  0.0 92.5 jit_solution(17293597246555497367)
XLA Ops:
  0.6 1.5 %copy.5.labels_ref = s32[256,1]{1,0:T(8,128)} copy(s32[256,1]{0,1:T(1,128)} %bitcast.2) | data formatting | bytes 2048 | tf_op jit(solution)/shard_map/broadcast_in_dim | solution.py:357
  2.1 86.9 %shard_map.50 = (f32[64,640]{1,0:T(8,128)}, f32[1,256,640]{2,1,0:T(8,128)}) custom-call(bf16[256,1024]{1,0:T(8,128)(2,1)} %x_ref.1, s32[256,1]{1,0:T(8,128)} %copy.5.labels_ref, f32[1024,1024]{1,0:T(8,128)} %bitcast.3), custom_call_target="tpu_custom_call" | custom-call | flops 2415919104 | bytes 6291456 | tf_op jit(solution)/shard_map/pallas_call | solution.py:317
  89.0 1.6 %copy.8 = f32[64,640]{1,0:T(8,128)} copy(f32[64,640]{1,0:T(8,128)} %get-tuple-element.4) | data formatting | bytes 327680
  90.6 2.0 %copy.9 = f32[1,256,640]{2,1,0:T(8,128)} copy(f32[1,256,640]{2,1,0:T(8,128)} %get-tuple-element.5) | data formatting | bytes 1310720

commit v3 on v2

--- a/solution.py
+++ b/solution.py
@@ -70,7 +70,7 @@
     def _():
         pl.semaphore_signal(barrier, inc=1, device_id=(feat - 1, me), device_id_type=MESH)
 
-    labels = labels_ref[...]
+    labels = jnp.broadcast_to(labels_ref[...], (CHUNK, rows)).T[:, 0:1]
     onehot = (labels == lax.broadcasted_iota(jnp.int32, (rows, C), 1)).astype(jnp.float32)
     cnt[0] = jnp.broadcast_to(jnp.sum(onehot, axis=0, keepdims=True), (8, C))
 
@@ -124,7 +124,7 @@
 
     def weights_of_rows():
         counts = count_outer()
-        hot = (labels_ref[...] == lax.broadcasted_iota(jnp.int32, (rows, C), 1)).astype(jnp.float32)
+        hot = (labels == lax.broadcasted_iota(jnp.int32, (rows, C), 1)).astype(jnp.float32)
         count_row = jnp.sum(hot * counts[0:1], axis=1, keepdims=True)
         row_weight[...] = total_rows / (C * count_row)
         scale[...] = jnp.ones_like(scale)
@@ -354,7 +354,7 @@
                 collective_id=0, has_side_effects=True, vmem_limit_bytes=60 * 1024 * 1024
             ),
             cost_estimate=pl.CostEstimate(flops=flops, bytes_accessed=6 << 20, transcendentals=0),
-        )(features, labels[:, None], inv_gram[0])
+        )(features, labels[None, :], inv_gram[0])
 
     in_specs = (P("rows", "feat"), P("rows"), P("feat", None, None))
     out_specs = (P(("feat", "rows"), None), P("feat", "rows", None))

time: 92.8 us -> 91.1 us (0.982)
  local copies, waits for them, and re-layouts: 5.03 us -> 3.56 us
    broadcast_in_dim x1 -> x0, local copies, waits for them, and re-layouts: 1.47 us -> none  [local(): labels[:, None]]
where the time goes in v3:
time: 91.1 us; the launch traced here: 90.9 us
  Pallas kernels  86.7 us (95%)
  local copies, waits for them, and re-layouts  3.56 us (4%)
    pallas_call x1, Pallas kernels, local(): pl.pallas_call(functools.partial(kernel, (n_feat, n_out, n_in), float(row...  86.7 us
    unnamed x2, local copies, waits for them, and re-layouts  3.56 us

profile of v3, /device:TPU:7, one launch (start us, length us, event | category | flops | bytes accessed | tf_op | source)
XLA Modules:
  0.0 90.9 jit_solution(7225721437532872374)
XLA Ops:
  0.6 86.7 %shard_map.50 = (f32[64,640]{1,0:T(8,128)}, f32[1,256,640]{2,1,0:T(8,128)}) custom-call(bf16[256,1024]{1,0:T(8,128)(2,1)} %x_ref.1, s32[1,256]{1,0:T(1,128)} %bitcast.3, f32[1024,1024]{1,0:T(8,128)} %bitcast.2), custom_call_target="tpu_custom_call" | custom-call | flops 2415919104 | bytes 6291456 | tf_op jit(solution)/shard_map/pallas_call | solution.py:317
  87.4 1.6 %copy.7 = f32[64,640]{1,0:T(8,128)} copy(f32[64,640]{1,0:T(8,128)} %get-tuple-element.4) | data formatting | bytes 327680
  89.0 2.0 %copy.8 = f32[1,256,640]{2,1,0:T(8,128)} copy(f32[1,256,640]{2,1,0:T(8,128)} %get-tuple-element.5) | data formatting | bytes 1310720
